TPU v7x, 32 devices: a whole 2x2x4 slice. The times are simulated.
32 devices in a mesh: grp: 2 (over y), sp: 4 (over z), flt: 2 (over x), rep: 2 (over core).
Axes of the slice: x: 2, y: 2, z: 4, core: 2. Of those that a mesh axis runs over, the one named last changes fastest.
Arguments:
- acts: float32 [64, 8, 8, 512], P(None, ('grp', 'sp'), ('flt', 'rep')), parts along dimension 1, may hold values from -6 to 6
- grad_out: float32 [64, 8, 8, 512], P(None, ('grp', 'sp'), ('flt', 'rep')), parts along dimension 1, may hold values from -6 to 6
- kernel: float32 [3, 3, 3, 64, 64], replicated, may hold values from -0.15625 to 0.15625
Outputs:
- input_grad: float32 [64, 8, 8, 512], P(None, ('grp', 'sp'), ('flt', 'rep')), parts along dimension 1
- weight_grad: float32 [6, 3, 3, 64, 64], P('grp'), parts along dimension 0
There are 2 independent parts, one for each index of `grp`. A program takes and returns all parts, laid end to end along the dimension named above; an argument that names none is the same for every part. Nothing has to cross between parts.
All inputs are finite; a program needn't handle non-finite values.
Results may differ from a plain program's by a relative error of at most 0.00007.
Values sent between devices are 32-bit elements; how exact they have to be, the bound alone decides.
A program may use at most 64 MiB of HBM per device.

v0:
```python
import math
import jax
import jax.numpy as jnp
from jax import lax
from jax.sharding import PartitionSpec as P


def padded_2(value, sides, width):
    for axis, dim in sides:
        count, length = (lax.axis_size(axis), value.shape[dim])
        up = [(i, (i + 1) % count) for i in range(count - 1)]
        down = [(j, i) for i, j in up]
        last = lax.slice_in_dim(value, length - width, length, axis=dim)
        first = lax.slice_in_dim(value, 0, width, axis=dim)
        before = lax.ppermute(last, axis, up)
        after = lax.ppermute(first, axis, down)
        value = jnp.concatenate([before, value, after], axis=dim)
    return value


def take_next(values):
    edge = jnp.zeros(values.shape[:-1] + (1,), values.dtype)
    return jnp.concatenate([values[..., 1:], edge], axis=-1)


def take_prior(values):
    edge = jnp.zeros(values.shape[:-1] + (1,), values.dtype)
    return jnp.concatenate([edge, values[..., :-1]], axis=-1)


def contract_last(left, right):
    return lax.dot_general(left, right, (((1,), (1,)), ((), ())), precision=lax.Precision.HIGHEST)


def per_device(acts, grad_out, kernel):
    cin = acts.shape[0]
    planes = acts.shape[1]
    rows = acts.shape[2]
    width = acts.shape[3]
    cout = grad_out.shape[0]
    voxels = (
        planes * lax.axis_size("sp") * rows * lax.axis_size("flt") * lax.axis_size("rep") * width
    )
    factor = 1.0 / math.sqrt(voxels)
    padded = padded_2(grad_out, (("sp", 1), (("flt", "rep"), 2)), 1)
    weights_tap = kernel.reshape(9, 3 * cin, cout)
    weight_terms = [jnp.zeros((3 * cin, cout), jnp.float32) for index in range(9)]
    source = acts[:, 0]
    source_stack = jnp.concatenate([take_prior(source), source, take_next(source)], axis=0).reshape(
        3 * cin, rows * width
    )
    partial_sum = jnp.zeros((3 * cin, rows * width), jnp.float32)
    for a_tap in range(3):
        for b_tap in range(3):
            index = 3 * a_tap + b_tap
            slab = padded[:, 2 - a_tap, 2 - b_tap : 2 - b_tap + rows, :].reshape(cout, rows * width)
            partial_sum = partial_sum + jnp.dot(
                weights_tap[index], slab, precision=lax.Precision.HIGHEST
            )
            weight_terms[index] = contract_last(source_stack, slab)
    parts_x = partial_sum.reshape(3, cin, rows, width)
    plane_out = take_next(parts_x[0]) + parts_x[1] + take_prior(parts_x[2])
    outputs = [plane_out]
    term = jnp.stack(weight_terms, axis=0).reshape(3, 3, 3, cin, cout) * factor
    weight_grad = lax.psum(term, ("sp", "flt", "rep"))
    input_grad = jnp.stack(outputs, axis=1)
    return (input_grad, weight_grad)


def solution(mesh):
    placed = (
        P(None, ("grp", "sp"), ("flt", "rep"), None),
        P(None, ("grp", "sp"), ("flt", "rep"), None),
        P(),
    )
    return jax.shard_map(
        per_device,
        mesh=mesh,
        in_specs=placed,
        out_specs=(P(None, ("grp", "sp"), ("flt", "rep"), None), P("grp", None, None, None, None)),
        check_vma=False,
    )
```

profile of v0, /device:TPU:0, one launch (start us, length us, event | category | flops | bytes accessed | tf_op | source)
XLA Modules:
  0.0 147.4 jit_solution(15860099137105820920)
XLA Ops:
  7.2 0.0 all-reduce.6.cloned.1.call-start
  7.2 1.0 copy.11
  8.2 0.0 copy-start.1
  8.2 5.1 %collective-permute-start = (f32[64,1,2,512]{3,0,2,1:T(8,128)S(1)}, f32[64,1,2,512]{3,0,2,1:T(8,128)S(1)}, u32[]{:S(2)}, u32[]{:S(2)}) collective-permute-start(f32[64,1,2,512]{3,0,2,1:T(8,128)S(1)} %copy.11), channel_id=1, source_target_pairs={{0,4},{4,8},{8,12},{1,5},{5,9},{9,13},{2,6},{6,10},{10,14},{3,7},{... | collective-permute-start | bytes 786440 | tf_op jit(solution)/shard_map/ppermute | solution.py:15
  13.3 1.3 collective-permute-start.1
  14.6 4.2 %collective-permute-done = f32[64,1,2,512]{3,0,2,1:T(8,128)S(1)} collective-permute-done((f32[64,1,2,512]{3,0,2,1:T(8,128)S(1)}, f32[64,1,2,512]{3,0,2,1:T(8,128)S(1)}, u32[]{:S(2)}, u32[]{:S(2)}) %collective-permute-start) | collective-permute-done | bytes 262176 | tf_op jit(solution)/shard_map/ppermute | solution.py:15
  18.9 0.0 copy-done.1
  18.9 4.0 %collective-permute-done.1 = f32[64,1,2,512]{3,0,2,1:T(8,128)S(1)} collective-permute-done((f32[64,1,2,512]{3,0,2,1:T(8,128)S(1)}, f32[64,1,2,512]{3,0,2,1:T(8,128)S(1)}, u32[]{:S(2)}, u32[]{:S(2)}) %collective-permute-start.1) | collective-permute-done | bytes 262176 | tf_op jit(solution)/shard_map/ppermute | solution.py:16
  23.0 0.0 copy-start
  23.0 0.1 fusion.15
  23.1 1.3 collective-permute-start.2
  24.4 3.1 %collective-permute-start.3 = (f32[64,3,1,512]{3,0,2,1:T(8,128)S(1)}, f32[64,3,1,512]{3,0,2,1:T(8,128)S(1)}, u32[]{:S(2)}, u32[]{:S(2)}) collective-permute-start(f32[64,3,1,512]{3,0,2,1:T(8,128)S(1)} %get-tuple-element.14), channel_id=1, source_target_pairs={{0,1},{1,2},{2,3},{4,5},{5,6},{6,7},{8,9},{9,10},{10,11},{12,13},{... | collective-permute-start | bytes 1179656 | tf_op jit(solution)/shard_map/ppermute | solution.py:15
  27.5 0.0 copy-done
  27.5 0.3 fusion.16
  27.8 0.3 concatenate.41
  28.2 0.1 concatenate.44
  28.5 0.2 copy.15
  28.8 0.2 copy.20
  29.1 0.0 collective-permute-done.2
  29.1 0.0 collective-permute-done.3
  29.1 0.1 pad_maximum_fusion
  29.2 0.2 copy.14
  29.5 0.2 copy.16
  29.8 0.2 copy.17
  30.0 0.2 copy.18
  30.3 0.2 copy.19
  30.6 0.2 copy.21
  30.9 0.9 fusion.13
  31.7 0.9 fusion.12
  32.6 0.9 fusion.11
  33.5 0.9 fusion.10
  34.4 0.9 fusion.9
  35.2 0.9 fusion.8
  36.1 0.9 fusion.7
  37.0 0.9 fusion.6
  37.9 0.9 fusion.5
  38.8 1.2 copy.22
  40.0 0.0 copy-start.2
  40.0 0.0 all-reduce.6.cloned.1.call-update
  40.1 1.1 copy-done.2
  41.2 0.8 convolution_bitcast_fusion.5
  42.0 0.8 convolution_add_fusion.2
  42.8 0.8 fusion.4
  43.5 0.8 fusion.3
  44.3 0.9 convolution_add_fusion.1
  45.3 0.8 fusion.2
  46.0 0.8 fusion.1
  46.8 0.8 convolution_add_fusion
  47.6 0.8 fusion
  48.4 0.1 fusion.14
  48.4 0.2 squeeze.48
  48.6 0.3 slice.117
  49.0 0.2 squeeze.50
  49.2 0.2 squeeze.49
  49.4 1.0 add_bitcast_fusion
  50.5 87.9 %all-reduce.6.cloned.1.call-done = f32[3,3,3,64,64]{4,3,2,1,0:T(8,128)} async-done(((f32[3,3,3,64,64]{4,3,2,1,0:T(8,128)}), f32[3,3,3,64,64]{4,3,2,1,0:T(8,128)}) %all-reduce.6.cloned.1.call-update) | async-done | bytes 442384 | tf_op jit(solution)/shard_map/psum | solution.py:65
  138.4 2.2 %copy.49 = f32[3,3,3,64,64]{4,3,2,1,0:T(8,128)} copy(f32[3,3,3,64,64]{4,3,2,1,0:T(8,128)} %all-reduce.6.cloned.1.call-done) | data formatting | bytes 884736
  (19 shorter events, 0.8 us)
Async XLA Ops:
  7.2 131.2 %all-reduce.6.cloned.1.call-start = ((), (), s32[]{:S(2)}) async-start(), calls=%async_computation | async-start | bytes 1769472 | tf_op jit(solution)/shard_map/psum | solution.py:65
  8.2 10.6 %copy-start.1 = (f32[64,1,2,512]{3,2,1,0:T(2,128)S(1)}, f32[64,1,2,512]{3,2,1,0:T(2,128)}, u32[]{:S(2)}) copy-start(f32[64,1,2,512]{3,2,1,0:T(2,128)} %param.4) | copy-start | bytes 786436
  8.2 10.6 %collective-permute-start = (f32[64,1,2,512]{3,0,2,1:T(8,128)S(1)}, f32[64,1,2,512]{3,0,2,1:T(8,128)S(1)}, u32[]{:S(2)}, u32[]{:S(2)}) collective-permute-start(f32[64,1,2,512]{3,0,2,1:T(8,128)S(1)} %copy.11), channel_id=1, source_target_pairs={{0,4},{4,8},{8,12},{1,5},{5,9},{9,13},{2,6},{6,10},{10,14},{3,7},{... | collective-permute-start | bytes 786440 | tf_op jit(solution)/shard_map/ppermute | solution.py:15
  13.3 9.7 %collective-permute-start.1 = (f32[64,1,2,512]{3,0,2,1:T(8,128)S(1)}, f32[64,1,2,512]{3,0,2,1:T(8,128)S(1)}, u32[]{:S(2)}, u32[]{:S(2)}) collective-permute-start(f32[64,1,2,512]{3,0,2,1:T(8,128)S(1)} %copy.11), channel_id=1, source_target_pairs={{4,0},{8,4},{12,8},{5,1},{9,5},{13,9},{6,2},{10,6},{14,10},{7,3},{... | collective-permute-start | bytes 786440 | tf_op jit(solution)/shard_map/ppermute | solution.py:16
  23.0 4.5 %copy-start = (f32[64,1,2,512]{3,2,1,0:T(2,128)S(1)}, f32[64,1,2,512]{3,2,1,0:T(2,128)}, u32[]{:S(2)}) copy-start(f32[64,1,2,512]{3,2,1,0:T(2,128)} %param.3) | copy-start | bytes 786436
  23.1 6.0 %collective-permute-start.2 = (f32[64,3,1,512]{3,0,2,1:T(8,128)S(1)}, f32[64,3,1,512]{3,0,2,1:T(8,128)S(1)}, u32[]{:S(2)}, u32[]{:S(2)}) collective-permute-start(f32[64,3,1,512]{3,0,2,1:T(8,128)S(1)} %get-tuple-element.15), channel_id=1, source_target_pairs={{1,0},{2,1},{3,2},{5,4},{6,5},{7,6},{9,8},{10,9},{11,10},{13,12},{... | collective-permute-start | bytes 1179656 | tf_op jit(solution)/shard_map/ppermute | solution.py:16
  24.4 4.7 %collective-permute-start.3 = (f32[64,3,1,512]{3,0,2,1:T(8,128)S(1)}, f32[64,3,1,512]{3,0,2,1:T(8,128)S(1)}, u32[]{:S(2)}, u32[]{:S(2)}) collective-permute-start(f32[64,3,1,512]{3,0,2,1:T(8,128)S(1)} %get-tuple-element.14), channel_id=1, source_target_pairs={{0,1},{1,2},{2,3},{4,5},{5,6},{6,7},{8,9},{9,10},{10,11},{12,13},{... | collective-permute-start | bytes 1179656 | tf_op jit(solution)/shard_map/ppermute | solution.py:15
  40.0 1.2 copy-start.2
Sparse Core Ops, SparseCore 0:
  40.2 98.1 all-reduce.5
where the time goes:
time: 148 us; the launch traced here: 147 us
  waiting for transfers between devices  96.2 us (65%)
  matrix products  15 us (10%)
  between operations  14.4 us (10%)
  starting transfers between devices  10.8 us (7%)
  local copies, waits for them, and re-layouts  9.81 us (7%)
    psum x1, waiting for transfers between devices, per_device(): weight_grad = lax.psum(term, ('sp', 'flt', 'rep'))  87.9 us
    ppermute x2, starting transfers between devices, padded_2(): before = lax.ppermute(last, axis, up)  8.13 us
    dot_general x9, matrix products, contract_last(): lax.dot_general(left, right, (((1,), (1,)), ((), ())), precision=lax.Prec...  7.91 us
    dot_general x9, matrix products, per_device(): jnp.dot(weights_tap[index], slab, precision=lax.Precision.HIGHEST)  7.09 us
    unnamed x24, local copies, waits for them, and re-layouts  5.03 us
    ppermute x2, waiting for transfers between devices, padded_2(): before = lax.ppermute(last, axis, up)  4.23 us
    ppermute x2, waiting for transfers between devices, padded_2(): after = lax.ppermute(first, axis, down)  4.05 us
  transfers between devices with their start and end apart: 5, of which 3 were waited for; matrix products, arithmetic and copies ran while one was open for 7% of the time, Pallas kernels for 0%

commit v1 on v0

--- a/solution.py
+++ b/solution.py
@@ -62,7 +62,7 @@
     plane_out = take_next(parts_x[0]) + parts_x[1] + take_prior(parts_x[2])
     outputs = [plane_out]
     term = jnp.stack(weight_terms, axis=0).reshape(3, 3, 3, cin, cout) * factor
-    weight_grad = lax.psum(term, ("sp", "flt", "rep"))
+    weight_grad = jnp.sum(lax.all_gather(term, ("sp", "flt", "rep")), axis=0)
     input_grad = jnp.stack(outputs, axis=1)
     return (input_grad, weight_grad)
 

time: 148 us -> 172 us (1.16)
  waiting for transfers between devices: 96.2 us -> 105 us
  matrix products: 15 us -> 23.1 us
  other arithmetic: 1.21 us -> 9.01 us
  starting transfers between devices: 10.8 us -> 8.88 us
    all_gather x0 -> x1, waiting for transfers between devices: none -> 97.7 us  [per_device(): weight_grad = jnp.sum(lax.all_gather(term, ('sp', 'flt', 'rep')), axis=0)]
    psum x1 -> x0, waiting for transfers between devices: 87.9 us -> none  [per_device(): weight_grad = lax.psum(term, ('sp', 'flt', 'rep'))]
    dot_general x9, matrix products: 7.09 us -> 15.2 us  [per_device(): jnp.dot(weights_tap[index], slab, precision=lax.Precision.HIGHEST)]
    reduce_sum x0 -> x1, other arithmetic: none -> 7.79 us  [per_device(): weight_grad = jnp.sum(lax.all_gather(term, ('sp', 'flt', 'rep')), axis=0)]
    ppermute x2, starting transfers between devices: 8.13 us -> 6.26 us  [padded_2(): before = lax.ppermute(last, axis, up)]
    unnamed x24 -> x17, local copies, waits for them, and re-layouts: 5.03 us -> 4.55 us
  transfers between devices with their start and end apart: 5 -> 5, of which waited for: 3 -> 3; matrix products, arithmetic and copies ran while one was open for 7% -> 13% of each run, Pallas kernels for 0% -> 0%
where the time goes in v1:
time: 172 us; the launch traced here: 171 us
  waiting for transfers between devices  105 us (61%)
  matrix products  23.1 us (13%)
  between operations  14.4 us (8%)
  local copies, waits for them, and re-layouts  10.4 us (6%)
  other arithmetic  9.01 us (5%)
  starting transfers between devices  8.88 us (5%)
    all_gather x1, waiting for transfers between devices, per_device(): weight_grad = jnp.sum(lax.all_gather(term, ('sp', 'flt', 'rep')), axis=0)  97.7 us
    dot_general x9, matrix products, per_device(): jnp.dot(weights_tap[index], slab, precision=lax.Precision.HIGHEST)  15.2 us
    dot_general x9, matrix products, contract_last(): lax.dot_general(left, right, (((1,), (1,)), ((), ())), precision=lax.Prec...  7.91 us
    reduce_sum x1, other arithmetic, per_device(): weight_grad = jnp.sum(lax.all_gather(term, ('sp', 'flt', 'rep')), axis=0)  7.79 us
    ppermute x2, starting transfers between devices, padded_2(): before = lax.ppermute(last, axis, up)  6.26 us
    unnamed x17, local copies, waits for them, and re-layouts  4.55 us
    ppermute x2, waiting for transfers between devices, padded_2(): before = lax.ppermute(last, axis, up)  4.23 us
  transfers between devices with their start and end apart: 5, of which 3 were waited for; matrix products, arithmetic and copies ran while one was open for 13% of the time, Pallas kernels for 0%

profile of v1, /device:TPU:0, one launch (start us, length us, event | category | flops | bytes accessed | tf_op | source)
XLA Modules:
  0.0 170.9 jit_solution(15440583459284702848)
XLA Ops:
  7.2 0.0 all-gather.2.cloned.1.call-start
  7.2 1.0 copy.10
  8.2 4.9 %collective-permute-start = (f32[64,1,2,512]{3,0,2,1:T(8,128)S(1)}, f32[64,1,2,512]{3,0,2,1:T(8,128)S(1)}, u32[]{:S(2)}, u32[]{:S(2)}) collective-permute-start(f32[64,1,2,512]{3,0,2,1:T(8,128)S(1)} %copy.10), channel_id=1, source_target_pairs={{0,4},{4,8},{8,12},{1,5},{5,9},{9,13},{2,6},{6,10},{10,14},{3,7},{... | collective-permute-start | bytes 786440 | tf_op jit(solution)/shard_map/ppermute | solution.py:15
  13.2 1.3 collective-permute-start.1
  14.5 4.2 %collective-permute-done = f32[64,1,2,512]{3,0,2,1:T(8,128)S(1)} collective-permute-done((f32[64,1,2,512]{3,0,2,1:T(8,128)S(1)}, f32[64,1,2,512]{3,0,2,1:T(8,128)S(1)}, u32[]{:S(2)}, u32[]{:S(2)}) %collective-permute-start) | collective-permute-done | bytes 262176 | tf_op jit(solution)/shard_map/ppermute | solution.py:15
  18.7 1.0 constant_dynamic-update-slice_fusion.1
  19.7 3.1 %collective-permute-done.1 = f32[64,1,2,512]{3,0,2,1:T(8,128)S(1)} collective-permute-done((f32[64,1,2,512]{3,0,2,1:T(8,128)S(1)}, f32[64,1,2,512]{3,0,2,1:T(8,128)S(1)}, u32[]{:S(2)}, u32[]{:S(2)}) %collective-permute-start.1) | collective-permute-done | bytes 262176 | tf_op jit(solution)/shard_map/ppermute | solution.py:16
  22.8 0.1 fusion.15
  22.9 1.3 collective-permute-start.3
  24.3 1.3 collective-permute-start.2
  25.6 1.4 fusion.16
  26.9 1.0 copy.26
  27.9 0.3 concatenate.41
  28.3 1.0 copy.32
  29.3 0.1 concatenate.44
  29.6 0.2 copy.14
  29.8 0.2 copy.19
  30.1 0.0 collective-permute-done.3
  30.1 0.0 collective-permute-done.2
  30.1 0.1 pad_maximum_fusion
  30.3 0.2 copy.13
  30.5 0.2 copy.15
  30.8 0.2 copy.16
  31.1 0.2 copy.17
  31.3 0.2 copy.18
  31.6 0.2 copy.20
  31.9 0.9 fusion.13
  32.7 0.9 fusion.12
  33.6 0.9 fusion.11
  34.5 0.9 fusion.10
  35.4 0.9 fusion.9
  36.3 0.9 fusion.8
  37.1 0.9 fusion.7
  38.0 0.9 fusion.6
  38.9 0.9 fusion.5
  39.8 1.2 copy.21
  41.1 0.0 all-gather.2.cloned.1.call-update
  41.1 1.7 convolution_bitcast_fusion.5
  42.7 1.7 convolution_add_fusion.2
  44.4 1.7 fusion.4
  46.1 1.7 fusion.3
  47.8 1.8 %convolution_add_fusion.1 = f32[192,1024]{1,0:T(8,128)S(1)} fusion(f32[192,1024]{1,0:T(8,128)S(1)} %fusion.3, f32[64,1024]{1,0:T(8,128)S(1)} %bitcast.167, f32[9,192,64]{2,1,0:T(8,128)} %bitcast.200), kind=kOutput, calls=%fused_computation.7 | convolution fusion | flops 151191552 | bytes 1933312 | tf_op jit(solution)/shard_map/dot_general | solution.py:57
  49.6 1.7 fusion.2
  51.3 1.7 fusion.1
  53.0 1.7 convolution_add_fusion
  54.6 1.7 %fusion = f32[192,1024]{1,0:T(8,128)S(1)} fusion(f32[192,1024]{1,0:T(8,128)S(1)} %convolution_add_fusion, f32[64,1024]{1,0:T(8,128)S(1)} %bitcast.175, f32[9,192,64]{2,1,0:T(8,128)} %bitcast.204), kind=kOutput, calls=%fused_computation.1 | convolution fusion | flops 151191552 | bytes 1933312 | tf_op jit(solution)/shard_map/dot_general | solution.py:57
  56.4 0.1 fusion.14
  56.4 0.2 squeeze.50
  56.6 0.2 squeeze.49
  56.9 0.2 squeeze.48
  57.1 0.3 slice.117
  57.4 1.0 add_bitcast_fusion
  58.5 97.7 %all-gather.2.cloned.1.call-done = f32[16,3,3,3,64,64]{5,4,3,2,1,0:T(8,128)} async-done(((f32[1,3,3,3,64,64]{5,4,3,2,1,0:T(8,128)}), f32[16,3,3,3,64,64]{5,4,3,2,1,0:T(8,128)}) %all-gather.2.cloned.1.call-update) | async-done | bytes 7077904 | tf_op jit(solution)/shard_map/all_gather | solution.py:65
  156.2 7.8 %reduce_sum.9 = f32[3,3,3,64,64]{4,3,2,1,0:T(8,128)} reduce(f32[16,3,3,3,64,64]{5,4,3,2,1,0:T(8,128)} %all-gather.2.cloned.1.call-done, f32[]{:T(128)} %constant.2.clone.1), dimensions={0}, to_apply=%region_0.0 | reduce | flops 1658880 | bytes 7520260 | tf_op jit(solution)/shard_map/reduce_sum | solution.py:65
  (16 shorter events, 0.6 us)
Async XLA Ops:
  7.2 149.1 %all-gather.2.cloned.1.call-start = ((), (), s32[]{:S(2)}) async-start(), calls=%async_computation | async-start | bytes 15040512 | tf_op jit(solution)/shard_map/all_gather | solution.py:65
  8.2 10.5 %collective-permute-start = (f32[64,1,2,512]{3,0,2,1:T(8,128)S(1)}, f32[64,1,2,512]{3,0,2,1:T(8,128)S(1)}, u32[]{:S(2)}, u32[]{:S(2)}) collective-permute-start(f32[64,1,2,512]{3,0,2,1:T(8,128)S(1)} %copy.10), channel_id=1, source_target_pairs={{0,4},{4,8},{8,12},{1,5},{5,9},{9,13},{2,6},{6,10},{10,14},{3,7},{... | collective-permute-start | bytes 786440 | tf_op jit(solution)/shard_map/ppermute | solution.py:15
  13.2 9.7 %collective-permute-start.1 = (f32[64,1,2,512]{3,0,2,1:T(8,128)S(1)}, f32[64,1,2,512]{3,0,2,1:T(8,128)S(1)}, u32[]{:S(2)}, u32[]{:S(2)}) collective-permute-start(f32[64,1,2,512]{3,0,2,1:T(8,128)S(1)} %copy.10), channel_id=1, source_target_pairs={{4,0},{8,4},{12,8},{5,1},{9,5},{13,9},{6,2},{10,6},{14,10},{7,3},{... | collective-permute-start | bytes 786440 | tf_op jit(solution)/shard_map/ppermute | solution.py:16
  22.9 7.2 %collective-permute-start.3 = (f32[64,3,1,512]{3,0,2,1:T(8,128)S(1)}, f32[64,3,1,512]{3,0,2,1:T(8,128)S(1)}, u32[]{:S(2)}, u32[]{:S(2)}) collective-permute-start(f32[64,3,1,512]{3,0,2,1:T(8,128)S(1)} %get-tuple-element.14), channel_id=1, source_target_pairs={{0,1},{1,2},{2,3},{4,5},{5,6},{6,7},{8,9},{9,10},{10,11},{12,13},{... | collective-permute-start | bytes 1179656 | tf_op jit(solution)/shard_map/ppermute | solution.py:15
  24.3 5.9 %collective-permute-start.2 = (f32[64,3,1,512]{3,0,2,1:T(8,128)S(1)}, f32[64,3,1,512]{3,0,2,1:T(8,128)S(1)}, u32[]{:S(2)}, u32[]{:S(2)}) collective-permute-start(f32[64,3,1,512]{3,0,2,1:T(8,128)S(1)} %get-tuple-element.15), channel_id=1, source_target_pairs={{1,0},{2,1},{3,2},{5,4},{6,5},{7,6},{9,8},{10,9},{11,10},{13,12},{... | collective-permute-start | bytes 1179656 | tf_op jit(solution)/shard_map/ppermute | solution.py:16
Sparse Core Ops, SparseCore 0:
  41.2 114.9 all-gather.1
